TPU v7x, 512 devices: a whole 4x4x16 slice. The times are simulated.
512 devices in a mesh: dp: 8 (over y, core), expert: 64 (over x, z).
Axes of the slice: x: 4, y: 4, z: 16, core: 2. Of those that a mesh axis runs over, the one named last changes fastest.
Arguments:
- activations: bfloat16 [1024, 8, 1536], P('expert', None, 'dp'), may hold values from -6 to 6
- w_down: bfloat16 [64, 1536, 4096], P('expert', 'dp'), may hold values from -0.15625 to 0.15625
- gate_weights: float32 [1024, 8], P('expert'), may hold values from 0.05 to 1
- cotangent: bfloat16 [1024, 4096], P('expert', 'dp'), may hold values from -0.59765625 to 0.59765625
- expert_ids: int32 [1024, 8], P('expert'), may hold values from 0 to 63, as said below
- replica_pick: int32 [1024, 8], P('expert'), may hold values from 0 to 1, as said below
- placement: int32 [16, 2], replicated, may hold values from 0 to 63, as said below
- group_cap: int32 [64], replicated, may hold values from 1 to 3, as said below
Outputs:
- combined: bfloat16 [1024, 4096], P('expert', 'dp')
- act_grad: bfloat16 [1024, 8, 1536], P('expert', None, 'dp')
- weight_grad: bfloat16 [64, 1536, 4096], P('expert', 'dp')
- gate_grad: float32 [1024, 8], P('expert')
Inputs may be any that keep to these rules, and one draw needn't show every extreme that they name: `expert_ids`: each row names 8 different experts. One expert, drawn from the seed and without a replica, is named by every token; replicated experts are named more often than the others. `replica_pick`: read only for rows whose expert has a replica. `placement`: column 0 holds distinct experts, column 1 distinct indices of expert; no index hosts a replica of the expert it owns, and no expert owned by a host is itself replicated. `group_cap`: the expert named by every token has its owner's entry equal to 3.
All inputs are finite; a program needn't handle non-finite values.
Results may differ from a plain program's by a relative error of at most 0.02.
Values may be sent and summed in bfloat16 or wider, within the bound.
No kernel may reach another device: no remote copies, remote signals or barrier semaphores. Data moves between devices by JAX's collectives and lax.ppermute only.
A program may use at most 64 MiB of HBM per device.

v0:
```python
import jax
import jax.numpy as jnp
from jax import lax
from jax.sharding import PartitionSpec as P


def routing_table(block_ids, block_pick, placement, group_cap):
    n_dev = group_cap.shape[0]
    flat_ids = block_ids.reshape(-1)
    flat_pick = block_pick.reshape(-1)
    match_copy = (flat_ids[:, None] == placement[None, :, 0]).astype(jnp.int32)
    has_copy = jnp.sum(match_copy, axis=1, dtype=jnp.int32)
    host_dev = jnp.sum(match_copy * placement[None, :, 1], axis=1, dtype=jnp.int32)
    to_copy = (has_copy > 0) & (flat_pick == 1)
    destination = jnp.where(to_copy, host_dev, flat_ids)
    row_kind = jnp.where(to_copy, 2, 1).astype(jnp.int32)
    onehot_dest = (destination[:, None] == jnp.arange(n_dev, dtype=jnp.int32)[None, :]).astype(
        jnp.int32
    )
    earlier = jnp.cumsum(onehot_dest, axis=0, dtype=jnp.int32) - onehot_dest
    row_rank = jnp.sum(earlier * onehot_dest, axis=1, dtype=jnp.int32)
    row_limit = jnp.sum(onehot_dest * group_cap[None, :], axis=1, dtype=jnp.int32)
    row_kept = row_rank < row_limit
    return (destination, row_kind, row_rank, row_kept)


def hosted(placement, n_dev):
    at_dev = (placement[:, 1][:, None] == jnp.arange(n_dev, dtype=jnp.int32)[None, :]).astype(
        jnp.int32
    )
    has_at = jnp.sum(at_dev, axis=0, dtype=jnp.int32)
    rep_at = jnp.sum(at_dev * placement[:, 0][:, None], axis=0, dtype=jnp.int32)
    return (has_at, rep_at)


def on_device(
    activations, w_down, gate_weights, cotangent, expert_ids, replica_pick, placement, group_cap
):
    n_dev = lax.axis_size("expert")
    tok_count, top_count, hidden_part = activations.shape
    width = w_down.shape[2]
    capacity = min(tok_count, 3 * tok_count * top_count // (2 * n_dev))
    slot_count = n_dev * capacity
    row_count = tok_count * top_count
    destination, row_kind, row_rank, row_kept = routing_table(
        expert_ids, replica_pick, placement, group_cap
    )
    slot_index = jnp.where(row_kept, destination * capacity + row_rank, slot_count)
    row_numbers = jnp.arange(row_count, dtype=jnp.int32)
    inverse = (
        jnp.full((slot_count + 1,), -1, jnp.int32).at[slot_index].set(row_numbers)[:slot_count]
    )
    slot_valid = inverse >= 0
    slot_rows = jnp.maximum(inverse, 0)
    slot_kind = jnp.where(slot_valid, jnp.take(row_kind, slot_rows, axis=0), 0).reshape(
        n_dev, capacity
    )
    safe_slot = jnp.minimum(slot_index, slot_count - 1)

    def to_slots(values):
        return jnp.where(
            slot_valid[:, None], jnp.take(values, slot_rows, axis=0), jnp.zeros((), values.dtype)
        )

    def to_rows(values):
        return jnp.where(
            row_kept[:, None], jnp.take(values, safe_slot, axis=0), jnp.zeros((), values.dtype)
        )

    has_at, rep_at = hosted(placement, n_dev)
    my_index = lax.axis_index("expert")
    is_host = jnp.take(has_at, my_index) > 0
    choose = (
        (has_at[:, None] > 0) & (rep_at[:, None] == jnp.arange(n_dev, dtype=jnp.int32)[None, :])
    ).astype(jnp.bfloat16)
    local_w = w_down[0]
    pieces = lax.all_to_all(local_w[None], "expert", split_axis=2, concat_axis=0, tiled=True)
    outgoing = jnp.einsum("de,ehc->dhc", choose, pieces, preferred_element_type=jnp.float32).astype(
        jnp.bfloat16
    )
    copy_w = lax.all_to_all(outgoing, "expert", split_axis=0, concat_axis=2, tiled=True)[0]
    flat_act = activations.reshape(row_count, hidden_part)
    sent = to_slots(flat_act).reshape(n_dev, capacity, hidden_part)
    arrived, arrived_kind = (
        lax.all_to_all(sent, "expert", split_axis=0, concat_axis=0, tiled=True),
        lax.all_to_all(slot_kind, "expert", split_axis=0, concat_axis=0, tiled=True),
    )
    inputs = arrived.reshape(slot_count, hidden_part)
    slot_kinds = arrived_kind.reshape(slot_count)
    own_mask = (slot_kinds == 1)[:, None]
    copy_mask = (slot_kinds == 2)[:, None]
    own_in = jnp.where(own_mask, inputs, jnp.zeros_like(inputs))
    copy_in = jnp.where(copy_mask, inputs, jnp.zeros_like(inputs))

    def forward_both(operands):
        return jnp.dot(operands[0], local_w, preferred_element_type=jnp.float32) + jnp.dot(
            operands[1], copy_w, preferred_element_type=jnp.float32
        )

    def forward_owned(operands):
        return jnp.dot(operands[0], local_w, preferred_element_type=jnp.float32)

    partial_value = lax.cond(is_host, forward_both, forward_owned, (own_in, copy_in))
    cotangent_full = lax.all_gather(cotangent, "dp", axis=1, tiled=True)
    returned = lax.all_to_all(
        partial_value.astype(jnp.bfloat16).reshape(n_dev, capacity, width),
        "expert",
        split_axis=0,
        concat_axis=0,
        tiled=True,
    )
    row_values = (
        to_rows(returned.reshape(slot_count, width))
        .astype(jnp.float32)
        .reshape(tok_count, top_count, width)
    )
    mixed_part = jnp.sum(gate_weights[:, :, None] * row_values, axis=1)
    combined = lax.psum_scatter(
        mixed_part.astype(jnp.bfloat16), "dp", scatter_dimension=1, tiled=True
    )
    gate_part = jnp.sum(cotangent_full.astype(jnp.float32)[:, None, :] * row_values, axis=2)
    gate_grad = lax.psum(gate_part, "dp")
    grad_tok = (
        (gate_weights[:, :, None] * cotangent_full.astype(jnp.float32)[:, None, :])
        .astype(jnp.bfloat16)
        .reshape(row_count, width)
    )
    grad_sent = to_slots(grad_tok).reshape(n_dev, capacity, width)
    grad_in = lax.all_to_all(grad_sent, "expert", split_axis=0, concat_axis=0, tiled=True)
    grad_in = grad_in.reshape(slot_count, width)

    def backward_both(operand):
        back_own = lax.dot_general(
            operand, local_w, (((1,), (1,)), ((), ())), preferred_element_type=jnp.float32
        )
        back_copy = lax.dot_general(
            operand, copy_w, (((1,), (1,)), ((), ())), preferred_element_type=jnp.float32
        )
        return jnp.where(own_mask, back_own, jnp.where(copy_mask, back_copy, 0.0)).astype(
            jnp.bfloat16
        )

    def backward_owned(operand):
        back_own = lax.dot_general(
            operand, local_w, (((1,), (1,)), ((), ())), preferred_element_type=jnp.float32
        )
        return jnp.where(own_mask, back_own, 0.0).astype(jnp.bfloat16)

    input_back = lax.cond(is_host, backward_both, backward_owned, grad_in)
    returned_grads = lax.all_to_all(
        input_back.reshape(n_dev, capacity, hidden_part),
        "expert",
        split_axis=0,
        concat_axis=0,
        tiled=True,
    )
    act_grad = to_rows(returned_grads.reshape(slot_count, hidden_part)).reshape(
        tok_count, top_count, hidden_part
    )
    own_grad = lax.dot_general(
        own_in, grad_in, (((0,), (0,)), ((), ())), preferred_element_type=jnp.float32
    )

    def copy_product(operands):
        return lax.dot_general(
            operands[0], operands[1], (((0,), (0,)), ((), ())), preferred_element_type=jnp.float32
        ).astype(jnp.bfloat16)

    def copy_nothing(operands):
        return jnp.zeros((operands[0].shape[1], operands[1].shape[1]), jnp.bfloat16)

    copy_grad = lax.cond(is_host, copy_product, copy_nothing, (copy_in, grad_in))
    grad_pieces = lax.all_to_all(copy_grad[None], "expert", split_axis=2, concat_axis=0, tiled=True)
    homeward = jnp.einsum(
        "de,dhc->ehc", choose, grad_pieces, preferred_element_type=jnp.float32
    ).astype(jnp.bfloat16)
    home_grad = lax.all_to_all(homeward, "expert", split_axis=0, concat_axis=2, tiled=True)[0]
    weight_grad = (own_grad + home_grad.astype(jnp.float32)).astype(jnp.bfloat16)[None]
    return (combined, act_grad, weight_grad, gate_grad)


def solution(mesh):
    return jax.shard_map(
        on_device,
        mesh=mesh,
        in_specs=(
            P("expert", None, "dp"),
            P("expert", "dp", None),
            P("expert", None),
            P("expert", "dp"),
            P("expert", None),
            P("expert", None),
            P(),
            P(),
        ),
        out_specs=(
            P("expert", "dp"),
            P("expert", None, "dp"),
            P("expert", "dp", None),
            P("expert", None),
        ),
        check_vma=False,
    )
```

profile of v0, /device:TPU:14, one launch (start us, length us, event | category | flops | bytes accessed | tf_op | source)
XLA Modules:
  0.0 808.6 jit_solution(3717038787633869883)
XLA Ops:
  7.2 9.9 %copy.94 = bf16[1,192,4096]{1,0,2:T(2,128)(2,1)} copy(bf16[1,192,4096]{2,1,0:T(8,128)(2,1)} %param.15) | data formatting | bytes 3145728 | tf_op args[1]
  17.6 23.5 %reduce.14 = bf16[4096,192]{1,0:T(8,128)(2,1)S(1)} reduce(bf16[4096,1,192]{2,1,0:T(2,128)(2,1)} %bitcast.115, bf16[]{:T(256)} %broadcast.341), dimensions={1}, to_apply=%bitcast.90.reduce_sub_computation | reduce | bytes 3145730
  41.1 3.3 reshape.474
  44.5 18.9 %all-to-all-start.2 = ((bf16[64,2,6144]{2,1,0:T(2,128)(2,1)}), bf16[64,2,6144]{2,1,0:T(2,128)(2,1)S(1)}, u32[]{:S(2)}, u32[]{:S(2)}) async-start(bf16[64,2,6144]{2,1,0:T(2,128)(2,1)} %reshape.474), calls=%async_computation.2 | async-start | bytes 3145728 | tf_op jit(solution)/shard_map/all_to_all | solution.py:77
  71.2 68.4 %all-to-all-done.2 = bf16[64,2,6144]{2,1,0:T(2,128)(2,1)S(1)} async-done(((bf16[64,2,6144]{2,1,0:T(2,128)(2,1)}), bf16[64,2,6144]{2,1,0:T(2,128)(2,1)S(1)}, u32[]{:S(2)}, u32[]{:S(2)}) %all-to-all-start.2) | async-done | bytes 1572896 | tf_op jit(solution)/shard_map/all_to_all | solution.py:77
  139.6 6.9 all-to-all-start
  146.5 7.2 reshape.475
  159.0 13.0 %all-to-all-start.1 = ((bf16[64,3,192]{2,1,0:T(4,128)(2,1)}), bf16[64,3,192]{2,1,0:T(4,128)(2,1)S(1)}, u32[]{:S(2)}, u32[]{:S(2)}) async-start(bf16[64,3,192]{2,1,0:T(4,128)(2,1)} %select_select_fusion.1), calls=%async_computation.1 | async-start | bytes 262144 | tf_op jit(solution)/shard_map/all_to_all | solution.py:85
  176.3 10.5 %all-to-all-done.1 = bf16[64,3,192]{2,1,0:T(4,128)(2,1)S(1)} async-done(((bf16[64,3,192]{2,1,0:T(4,128)(2,1)}), bf16[64,3,192]{2,1,0:T(4,128)(2,1)S(1)}, u32[]{:S(2)}, u32[]{:S(2)}) %all-to-all-start.1) | async-done | bytes 73760 | tf_op jit(solution)/shard_map/all_to_all | solution.py:85
  186.8 6.7 all-to-all-start.3
  195.5 95.2 %all-to-all-done.3 = bf16[64,192,64]{1,2,0:T(8,128)(2,1)} async-done(((bf16[64,192,64]{1,2,0:T(8,128)(2,1)}), bf16[64,192,64]{1,2,0:T(8,128)(2,1)}, u32[]{:S(2)}, u32[]{:S(2)}) %all-to-all-start.3) | async-done | bytes 1572896 | tf_op jit(solution)/shard_map/all_to_all | solution.py:81
  293.7 9.9 %all-to-all-start.4 = ((bf16[64,3,4096]{2,1,0:T(4,128)(2,1)}), bf16[64,3,4096]{2,1,0:T(4,128)(2,1)}, u32[]{:S(2)}, u32[]{:S(2)}) async-start(bf16[64,3,4096]{2,1,0:T(4,128)(2,1)} %reshape.365), calls=%async_computation.4 | async-start | bytes 4194304 | tf_op jit(solution)/shard_map/all_to_all | solution.py:105
  304.4 13.0 %all_gather.3 = bf16[16,4096]{1,0:T(8,128)(2,1)S(1)} all-gather(bf16[16,512]{1,0:T(8,128)(2,1)S(1)} %copy-done.17), channel_id=1, replica_groups=mesh['dp'=8,'expert'=64] {'dp'}, dimensions={1}, use_global_device_ids=true | all-gather | bytes 147456 | tf_op jit(solution)/shard_map/all_gather | solution.py:104
  317.4 84.0 %all-to-all-done.4 = bf16[64,3,4096]{2,1,0:T(4,128)(2,1)} async-done(((bf16[64,3,4096]{2,1,0:T(4,128)(2,1)}), bf16[64,3,4096]{2,1,0:T(4,128)(2,1)}, u32[]{:S(2)}, u32[]{:S(2)}) %all-to-all-start.4) | async-done | bytes 1572896 | tf_op jit(solution)/shard_map/all_to_all | solution.py:105
  401.4 3.1 reshape.366
  406.3 2.8 gather_fusion.3
  409.1 2.8 gather.39
  414.3 7.4 all-to-all-start.5
  421.8 97.1 %all-to-all-done.5 = bf16[64,3,4096]{2,1,0:T(4,128)(2,1)S(1)} async-done(((bf16[64,3,4096]{2,1,0:T(4,128)(2,1)}), bf16[64,3,4096]{2,1,0:T(4,128)(2,1)S(1)}, u32[]{:S(2)}, u32[]{:S(2)}) %all-to-all-start.5) | async-done | bytes 1572896 | tf_op jit(solution)/shard_map/all_to_all | solution.py:129
  522.6 9.9 %copy.105 = bf16[1,192,4096]{1,0,2:T(2,128)(2,1)} copy(bf16[1,192,4096]{2,1,0:T(8,128)(2,1)} %bitcast.125) | data formatting | bytes 3145728 | tf_op jit(solution)/shard_map/broadcast_in_dim | solution.py:173
  532.5 24.9 %reduce.15 = bf16[4096,192]{1,0:T(8,128)(2,1)} reduce(bf16[4096,1,192]{2,1,0:T(2,128)(2,1)} %bitcast.116, bf16[]{:T(256)} %broadcast.341), dimensions={1}, to_apply=%bitcast.92.reduce_sub_computation | reduce | bytes 3145730
  557.4 5.5 reshape.476
  563.0 10.6 %all-to-all-start.7 = ((bf16[64,2,6144]{2,1,0:T(2,128)(2,1)}), bf16[64,2,6144]{2,1,0:T(2,128)(2,1)}, u32[]{:S(2)}, u32[]{:S(2)}) async-start(bf16[64,2,6144]{2,1,0:T(2,128)(2,1)} %reshape.476), calls=%async_computation.8 | async-start | bytes 3145728 | tf_op jit(solution)/shard_map/all_to_all | solution.py:173
  579.9 69.3 %all-to-all-done.7 = bf16[64,2,6144]{2,1,0:T(2,128)(2,1)} async-done(((bf16[64,2,6144]{2,1,0:T(2,128)(2,1)}), bf16[64,2,6144]{2,1,0:T(2,128)(2,1)}, u32[]{:S(2)}, u32[]{:S(2)}) %all-to-all-start.7) | async-done | bytes 1572896 | tf_op jit(solution)/shard_map/all_to_all | solution.py:173
  649.2 7.3 all-to-all-start.6
  656.5 10.7 %reshape.477 = bf16[4096,1,192]{2,1,0:T(2,128)(2,1)} reshape(bf16[64,2,6144]{2,1,0:T(2,128)(2,1)} %all-to-all-done.7) | data formatting | bytes 3145728
  674.0 15.5 %all-to-all-start.8 = ((bf16[64,192,64]{1,2,0:T(8,128)(2,1)}), bf16[64,192,64]{1,2,0:T(8,128)(2,1)}, u32[]{:S(2)}, u32[]{:S(2)}) async-start(bf16[64,192,64]{1,2,0:T(8,128)(2,1)} %copy.107), calls=%async_computation.9 | async-start | bytes 4194304 | tf_op jit(solution)/shard_map/all_to_all | solution.py:177
  692.3 11.3 %psum.7 = f32[16,8]{1,0:T(8,128)S(1)} all-reduce(f32[16,8]{1,0:T(8,128)S(1)} %reduce_sum.100), channel_id=1, replica_groups=mesh['dp'=8,'expert'=64] {'dp'}, use_global_device_ids=true, to_apply=%region_17.18 | all-reduce | flops 128 | bytes 1024 | tf_op jit(solution)/shard_map/psum | solution.py:122
  705.9 81.1 %all-to-all-done.8 = bf16[64,192,64]{1,2,0:T(8,128)(2,1)} async-done(((bf16[64,192,64]{1,2,0:T(8,128)(2,1)}), bf16[64,192,64]{1,2,0:T(8,128)(2,1)}, u32[]{:S(2)}, u32[]{:S(2)}) %all-to-all-start.8) | async-done | bytes 1572896 | tf_op jit(solution)/shard_map/all_to_all | solution.py:177
  786.9 4.1 bitcast_convert_fusion
  791.0 5.3 copy.108
  796.4 5.1 fusion.2
  (157 shorter events, 53.1 us)
Async XLA Ops:
  7.2 62.0 %copy-start = (bf16[16,8,192]{2,1,0:T(8,128)(2,1)S(1)}, bf16[16,8,192]{2,1,0:T(8,128)(2,1)}, u32[]{:S(2)}) copy-start(bf16[16,8,192]{2,1,0:T(8,128)(2,1)} %param.14) | copy-start | bytes 147460
  44.5 19.0 %copy-start.29 = (s32[16,8]{0,1:T(8,128)S(1)}, s32[16,8]{0,1:T(8,128)}, u32[]{:S(2)}) copy-start(s32[16,8]{0,1:T(8,128)} %param.18) | copy-start | bytes 1540
  44.5 19.2 %copy-start.30 = (s32[16,8]{0,1:T(8,128)S(1)}, s32[16,8]{0,1:T(8,128)}, u32[]{:S(2)}) copy-start(s32[16,8]{0,1:T(8,128)} %param.19) | copy-start | bytes 1540
  44.5 19.5 %copy-start.35 = (s32[16,2]{0,1:T(2,128)S(1)}, s32[16,2]{0,1:T(2,128)}, u32[]{:S(2)}) copy-start(s32[16,2]{0,1:T(2,128)} %param.20) | copy-start | bytes 388
  44.5 20.2 %copy-start.36 = (s32[64]{0:T(128)S(1)}, s32[64]{0:T(128)}, u32[]{:S(2)}) copy-start(s32[64]{0:T(128)} %param.21) | copy-start | bytes 772
  44.5 95.1 %all-to-all-start.2 = ((bf16[64,2,6144]{2,1,0:T(2,128)(2,1)}), bf16[64,2,6144]{2,1,0:T(2,128)(2,1)S(1)}, u32[]{:S(2)}, u32[]{:S(2)}) async-start(bf16[64,2,6144]{2,1,0:T(2,128)(2,1)} %reshape.474), calls=%async_computation.2 | async-start | bytes 3145728 | tf_op jit(solution)/shard_map/all_to_all | solution.py:77
  68.3 85.4 %copy-start.7 = (pred[64,3]{1,0:T(8,128)(4,1)}, pred[64,3]{1,0:T(8,128)(4,1)S(1)}, u32[]{:S(2)}) copy-start(pred[64,3]{1,0:T(8,128)(4,1)S(1)} %le.50) | copy-start | bytes 580
  70.3 101.7 %copy-start.21 = (s32[64]{0:T(128)}, s32[64]{0:T(128)S(1)}, u32[]{:S(2)}) copy-start(s32[64]{0:T(128)S(1)} %get-tuple-element.144) | copy-start | bytes 772
  139.6 19.4 %all-to-all-start = ((s32[64,1,3]{2,1,0:T(1,128)}), s32[64,1,3]{2,1,0:T(1,128)S(1)}, u32[]{:S(2)}, u32[]{:S(2)}) async-start(s32[64,1,3]{2,1,0:T(1,128)} %bitcast.9), calls=%async_computation | async-start | bytes 65536 | tf_op jit(solution)/shard_map/all_to_all | solution.py:86
  146.5 25.5 %copy-start.32 = (pred[64]{0:T(512)(128)(4,1)}, pred[64]{0:T(512)(128)(4,1)S(1)}, u32[]{:S(2)}) copy-start(pred[64]{0:T(512)(128)(4,1)S(1)} %broadcast_compare_fusion.4) | copy-start | bytes 196
  159.0 27.8 %all-to-all-start.1 = ((bf16[64,3,192]{2,1,0:T(4,128)(2,1)}), bf16[64,3,192]{2,1,0:T(4,128)(2,1)S(1)}, u32[]{:S(2)}, u32[]{:S(2)}) async-start(bf16[64,3,192]{2,1,0:T(4,128)(2,1)} %select_select_fusion.1), calls=%async_computation.1 | async-start | bytes 262144 | tf_op jit(solution)/shard_map/all_to_all | solution.py:85
  176.2 114.5 %copy-start.2 = (bf16[1,192,4096]{2,1,0:T(8,128)(2,1)S(1)}, bf16[1,192,4096]{2,1,0:T(8,128)(2,1)}, u32[]{:S(2)}) copy-start(bf16[1,192,4096]{2,1,0:T(8,128)(2,1)} %param.15) | copy-start | bytes 4718596
  186.8 103.9 %all-to-all-start.3 = ((bf16[64,192,64]{1,2,0:T(8,128)(2,1)}), bf16[64,192,64]{1,2,0:T(8,128)(2,1)}, u32[]{:S(2)}, u32[]{:S(2)}) async-start(bf16[64,192,64]{1,2,0:T(8,128)(2,1)} %copy.97), calls=%async_computation.3 | async-start | bytes 4194304 | tf_op jit(solution)/shard_map/all_to_all | solution.py:81
  293.6 10.1 %copy-start.24 = (s32[128]{0:T(128)S(1)}, s32[128]{0:T(128)}, u32[]{:S(2)}) copy-start(s32[128]{0:T(128)} %copy-done.23) | copy-start | bytes 1540
  293.6 10.2 %copy-start.28 = (s32[128]{0:T(128)S(1)}, s32[128]{0:T(128)}, u32[]{:S(2)}) copy-start(s32[128]{0:T(128)} %copy-done.27) | copy-start | bytes 1540
  293.6 10.3 %copy-start.31 = (f32[16,8]{0,1:T(8,128)S(1)}, f32[16,8]{0,1:T(8,128)}, u32[]{:S(2)}) copy-start(f32[16,8]{0,1:T(8,128)} %param.16) | copy-start | bytes 1540
  293.6 10.5 %copy-start.12 = (s32[16,8]{1,0:T(8,128)S(1)}, s32[16,8]{1,0:T(8,128)}, u32[]{:S(2)}) copy-start(s32[16,8]{1,0:T(8,128)} %copy-done.11) | copy-start | bytes 1540
  293.6 10.7 %copy-start.17 = (bf16[16,512]{1,0:T(8,128)(2,1)S(1)}, bf16[16,512]{1,0:T(8,128)(2,1)}, u32[]{:S(2)}) copy-start(bf16[16,512]{1,0:T(8,128)(2,1)} %param.17) | copy-start | bytes 49156
  293.7 23.7 %copy-start.34 = (s32[128]{0:T(128)S(1)}, s32[128]{0:T(128)}, u32[]{:S(2)}) copy-start(s32[128]{0:T(128)} %get-tuple-element.150) | copy-start | bytes 1540
  293.7 107.7 %all-to-all-start.4 = ((bf16[64,3,4096]{2,1,0:T(4,128)(2,1)}), bf16[64,3,4096]{2,1,0:T(4,128)(2,1)}, u32[]{:S(2)}, u32[]{:S(2)}) async-start(bf16[64,3,4096]{2,1,0:T(4,128)(2,1)} %reshape.365), calls=%async_computation.4 | async-start | bytes 4194304 | tf_op jit(solution)/shard_map/all_to_all | solution.py:105
  304.0 100.5 %copy-start.9 = (f32[16,8]{1,0:T(8,128)}, f32[16,8]{1,0:T(8,128)S(1)}, u32[]{:S(2)}) copy-start(f32[16,8]{1,0:T(8,128)S(1)} %copy.88) | copy-start | bytes 1540
  304.2 100.4 %copy-start.13 = (pred[16,8]{1,0:T(8,128)(4,1)}, pred[16,8]{1,0:T(8,128)(4,1)S(1)}, u32[]{:S(2)}) copy-start(pred[16,8]{1,0:T(8,128)(4,1)S(1)} %get-tuple-element.148) | copy-start | bytes 388
  304.2 100.4 %copy-start.15 = (pred[16,8]{1,0:T(8,128)(4,1)}, pred[16,8]{1,0:T(8,128)(4,1)S(1)}, u32[]{:S(2)}) copy-start(pred[16,8]{1,0:T(8,128)(4,1)S(1)} %get-tuple-element.149) | copy-start | bytes 388
  414.3 104.5 %all-to-all-start.5 = ((bf16[64,3,4096]{2,1,0:T(4,128)(2,1)}), bf16[64,3,4096]{2,1,0:T(4,128)(2,1)S(1)}, u32[]{:S(2)}, u32[]{:S(2)}) async-start(bf16[64,3,4096]{2,1,0:T(4,128)(2,1)} %select_select_fusion), calls=%async_computation.6 | async-start | bytes 4194304 | tf_op jit(solution)/shard_map/all_to_all | solution.py:129
  563.0 86.2 %all-to-all-start.7 = ((bf16[64,2,6144]{2,1,0:T(2,128)(2,1)}), bf16[64,2,6144]{2,1,0:T(2,128)(2,1)}, u32[]{:S(2)}, u32[]{:S(2)}) async-start(bf16[64,2,6144]{2,1,0:T(2,128)(2,1)} %reshape.476), calls=%async_computation.8 | async-start | bytes 3145728 | tf_op jit(solution)/shard_map/all_to_all | solution.py:173
  649.2 24.8 %all-to-all-start.6 = ((bf16[64,3,192]{2,1,0:T(4,128)(2,1)}), bf16[64,3,192]{2,1,0:T(4,128)(2,1)S(1)}, u32[]{:S(2)}, u32[]{:S(2)}) async-start(bf16[64,3,192]{2,1,0:T(4,128)(2,1)} %reshape.369), calls=%async_computation.7 | async-start | bytes 262144 | tf_op jit(solution)/shard_map/all_to_all | solution.py:150
  674.0 16.6 %copy-start.10 = (f32[16,8]{1,0:T(8,128)S(1)}, f32[16,8]{1,0:T(8,128)}, u32[]{:S(2)}) copy-start(f32[16,8]{1,0:T(8,128)} %copy-done.9) | copy-start | bytes 1540
  674.0 16.6 %copy-start.14 = (pred[16,8]{1,0:T(8,128)(4,1)S(1)}, pred[16,8]{1,0:T(8,128)(4,1)}, u32[]{:S(2)}) copy-start(pred[16,8]{1,0:T(8,128)(4,1)} %copy-done.13) | copy-start | bytes 388
  674.0 16.6 %copy-start.16 = (pred[16,8]{1,0:T(8,128)(4,1)S(1)}, pred[16,8]{1,0:T(8,128)(4,1)}, u32[]{:S(2)}) copy-start(pred[16,8]{1,0:T(8,128)(4,1)} %copy-done.15) | copy-start | bytes 388
  674.0 113.0 %all-to-all-start.8 = ((bf16[64,192,64]{1,2,0:T(8,128)(2,1)}), bf16[64,192,64]{1,2,0:T(8,128)(2,1)}, u32[]{:S(2)}, u32[]{:S(2)}) async-start(bf16[64,192,64]{1,2,0:T(8,128)(2,1)} %copy.107), calls=%async_computation.9 | async-start | bytes 4194304 | tf_op jit(solution)/shard_map/all_to_all | solution.py:177
  689.4 112.1 %reduce-scatter.2.cloned.1.call-start = ((), (), s32[]{:S(2)}) async-start(), calls=%async_computation.10 | async-start | bytes 147456 | tf_op jit(solution)/shard_map/reduce_scatter | solution.py:118
  791.0 10.5 %copy-start.1 = (bf16[16,8,192]{2,1,0:T(8,128)(2,1)S(1)}, bf16[16,8,192]{2,1,0:T(8,128)(2,1)}, u32[]{:S(2)}) copy-start(bf16[16,8,192]{2,1,0:T(8,128)(2,1)} %param.14) | copy-start | bytes 147460
  (13 other events, 55.8 us)
Sparse Core Ops, SparseCore 0:
  693.6 36.2 reduce-scatter.1
where the time goes:
time: 819 us; the launch traced here: 809 us
  waiting for transfers between devices  508 us (62%)
  starting transfers between devices  96.3 us (12%)
  local copies, waits for them, and re-layouts  89.6 us (11%)
  other arithmetic  63 us (8%)
  blocking collectives  24.3 us (3%)
  between operations  15.6 us (2%)
  matrix products  11.6 us (1%)
    all_to_all x1, waiting for transfers between devices, on_device(): lax.all_to_all(grad_sent, 'expert', split_axis=0, concat_axis=0, tiled=True)  97.1 us
    all_to_all x1, waiting for transfers between devices, on_device(): lax.all_to_all(outgoing, 'expert', split_axis=0, concat_axis=2, tiled=True)  95.2 us
    all_to_all x1, waiting for transfers between devices, on_device(): lax.all_to_all(partial_value.astype(jnp.bfloat16).reshape(n_dev, capacity...  84 us
    all_to_all x1, waiting for transfers between devices, on_device(): lax.all_to_all(homeward, 'expert', split_axis=0, concat_axis=2, tiled=True)  81.1 us
    all_to_all x1, waiting for transfers between devices, on_device(): lax.all_to_all(copy_grad[None], 'expert', split_axis=2, concat_axis=0, ti...  69.3 us
    all_to_all x1, waiting for transfers between devices, on_device(): lax.all_to_all(local_w[None], 'expert', split_axis=2, concat_axis=0, tile...  68.4 us
    unnamed x2, other arithmetic  48.5 us
    unnamed x82, local copies, waits for them, and re-layouts  44.1 us
  transfers between devices with their start and end apart: 10, of which 8 were waited for; matrix products, arithmetic and copies ran while one was open for 8% of the time, Pallas kernels for 0%

commit v1 on v0

--- a/solution.py
+++ b/solution.py
@@ -2,6 +2,14 @@
 import jax.numpy as jnp
 from jax import lax
 from jax.sharding import PartitionSpec as P
+
+
+def sites_state(array_here, link_axis):
+    upper = jnp.split(array_here, lax.axis_size(link_axis), axis=0)
+    left_arr = jnp.stack(upper)
+    return jnp.concatenate(
+        lax.all_to_all(left_arr, axis_name=link_axis, split_axis=0, concat_axis=0), axis=2
+    )
 
 
 def routing_table(block_ids, block_pick, placement, group_cap):
@@ -78,7 +86,7 @@
     outgoing = jnp.einsum("de,ehc->dhc", choose, pieces, preferred_element_type=jnp.float32).astype(
         jnp.bfloat16
     )
-    copy_w = lax.all_to_all(outgoing, "expert", split_axis=0, concat_axis=2, tiled=True)[0]
+    copy_w = sites_state(outgoing, "expert")[0]
     flat_act = activations.reshape(row_count, hidden_part)
     sent = to_slots(flat_act).reshape(n_dev, capacity, hidden_part)
     arrived, arrived_kind = (

time: 819 us -> 864 us (1.055)
  local copies, waits for them, and re-layouts: 89.6 us -> 137 us
    unnamed x82 -> x146, local copies, waits for them, and re-layouts: 44.1 us -> 82.5 us
  transfers between devices with their start and end apart: 10 -> 10, of which waited for: 8 -> 7; matrix products, arithmetic and copies ran while one was open for 8% -> 13% of each run, Pallas kernels for 0% -> 0%
where the time goes in v1:
time: 864 us; the launch traced here: 855 us
  waiting for transfers between devices  509 us (59%)
  local copies, waits for them, and re-layouts  137 us (16%)
  starting transfers between devices  98.8 us (11%)
  other arithmetic  59 us (7%)
  blocking collectives  24.4 us (3%)
  between operations  15.6 us (2%)
  matrix products  11.6 us (1%)
    all_to_all x1, waiting for transfers between devices, on_device(): lax.all_to_all(grad_sent, 'expert', split_axis=0, concat_axis=0, tiled=True)  97.1 us
    all_to_all x1, waiting for transfers between devices, sites_state(): lax.all_to_all(left_arr, axis_name=link_axis, split_axis=0, concat_axis=0)  95.2 us
    all_to_all x1, waiting for transfers between devices, on_device(): lax.all_to_all(partial_value.astype(jnp.bfloat16).reshape(n_dev, capacity...  83.7 us
    unnamed x146, local copies, waits for them, and re-layouts  82.5 us
    all_to_all x1, waiting for transfers between devices, on_device(): lax.all_to_all(homeward, 'expert', split_axis=0, concat_axis=2, tiled=True)  81.1 us
    all_to_all x1, waiting for transfers between devices, on_device(): lax.all_to_all(copy_grad[None], 'expert', split_axis=2, concat_axis=0, ti...  69.3 us
    all_to_all x1, waiting for transfers between devices, on_device(): lax.all_to_all(local_w[None], 'expert', split_axis=2, concat_axis=0, tile...  68.5 us
    unnamed x2, other arithmetic  48.6 us
  transfers between devices with their start and end apart: 10, of which 7 were waited for; matrix products, arithmetic and copies ran while one was open for 13% of the time, Pallas kernels for 0%

profile of v1, /device:TPU:14, one launch (start us, length us, event | category | flops | bytes accessed | tf_op | source)
XLA Modules:
  0.0 855.3 jit_solution(6218903319753352295)
XLA Ops:
  7.2 9.9 %copy.2193 = bf16[1,192,4096]{1,0,2:T(2,128)(2,1)} copy(bf16[1,192,4096]{2,1,0:T(8,128)(2,1)} %param.15) | data formatting | bytes 3145728 | tf_op args[1]
  17.6 23.6 %reduce.14 = bf16[4096,192]{1,0:T(8,128)(2,1)S(1)} reduce(bf16[4096,1,192]{2,1,0:T(2,128)(2,1)} %bitcast.243, bf16[]{:T(256)} %broadcast.341), dimensions={1}, to_apply=%bitcast.216.reduce_sub_computation | reduce | bytes 3145730
  41.3 3.3 reshape.477
  44.6 18.9 %all-to-all-start.2 = ((bf16[64,2,6144]{2,1,0:T(2,128)(2,1)}), bf16[64,2,6144]{2,1,0:T(2,128)(2,1)S(1)}, u32[]{:S(2)}, u32[]{:S(2)}) async-start(bf16[64,2,6144]{2,1,0:T(2,128)(2,1)} %reshape.477), calls=%async_computation.2 | async-start | bytes 3145728 | tf_op jit(solution)/shard_map/all_to_all | solution.py:85
  71.2 68.5 %all-to-all-done.2 = bf16[64,2,6144]{2,1,0:T(2,128)(2,1)S(1)} async-done(((bf16[64,2,6144]{2,1,0:T(2,128)(2,1)}), bf16[64,2,6144]{2,1,0:T(2,128)(2,1)S(1)}, u32[]{:S(2)}, u32[]{:S(2)}) %all-to-all-start.2) | async-done | bytes 1572896 | tf_op jit(solution)/shard_map/all_to_all | solution.py:85
  139.7 7.2 all-to-all-start
  146.9 7.2 reshape.478
  200.5 15.1 %all-to-all-start.1 = ((bf16[64,3,192]{2,1,0:T(4,128)(2,1)}), bf16[64,3,192]{2,1,0:T(4,128)(2,1)S(1)}, u32[]{:S(2)}, u32[]{:S(2)}) async-start(bf16[64,3,192]{2,1,0:T(4,128)(2,1)} %select_select_fusion.1), calls=%async_computation.1 | async-start | bytes 262144 | tf_op jit(solution)/shard_map/all_to_all | solution.py:93
  216.8 13.7 %all-to-all-done.1 = bf16[64,3,192]{2,1,0:T(4,128)(2,1)S(1)} async-done(((bf16[64,3,192]{2,1,0:T(4,128)(2,1)}), bf16[64,3,192]{2,1,0:T(4,128)(2,1)S(1)}, u32[]{:S(2)}, u32[]{:S(2)}) %all-to-all-start.1) | async-done | bytes 73760 | tf_op jit(solution)/shard_map/all_to_all | solution.py:93
  230.5 6.7 all-to-all-start.3
  239.2 95.2 %all-to-all-done.3 = bf16[64,1,192,64]{2,3,1,0:T(8,128)(2,1)} async-done(((bf16[64,1,192,64]{2,3,1,0:T(8,128)(2,1)}), bf16[64,1,192,64]{2,3,1,0:T(8,128)(2,1)}, u32[]{:S(2)}, u32[]{:S(2)}) %all-to-all-start.3) | async-done | bytes 1572896 | tf_op jit(solution)/shard_map/all_to_all | solution.py:11
  337.4 10.3 %all-to-all-start.4 = ((bf16[64,3,4096]{2,1,0:T(4,128)(2,1)}), bf16[64,3,4096]{2,1,0:T(4,128)(2,1)}, u32[]{:S(2)}, u32[]{:S(2)}) async-start(bf16[64,3,4096]{2,1,0:T(4,128)(2,1)} %reshape.368), calls=%async_computation.4 | async-start | bytes 4194304 | tf_op jit(solution)/shard_map/all_to_all | solution.py:113
  348.5 13.0 %all_gather.3 = bf16[16,4096]{1,0:T(8,128)(2,1)S(1)} all-gather(bf16[16,512]{1,0:T(8,128)(2,1)S(1)} %copy-done.17), channel_id=1, replica_groups=mesh['dp'=8,'expert'=64] {'dp'}, dimensions={1}, use_global_device_ids=true | all-gather | bytes 147456 | tf_op jit(solution)/shard_map/all_gather | solution.py:112
  361.5 83.7 %all-to-all-done.4 = bf16[64,3,4096]{2,1,0:T(4,128)(2,1)} async-done(((bf16[64,3,4096]{2,1,0:T(4,128)(2,1)}), bf16[64,3,4096]{2,1,0:T(4,128)(2,1)}, u32[]{:S(2)}, u32[]{:S(2)}) %all-to-all-start.4) | async-done | bytes 1572896 | tf_op jit(solution)/shard_map/all_to_all | solution.py:113
  445.3 3.1 reshape.369
  450.2 2.8 gather_fusion.3
  458.2 7.5 all-to-all-start.5
  465.7 97.1 %all-to-all-done.5 = bf16[64,3,4096]{2,1,0:T(4,128)(2,1)S(1)} async-done(((bf16[64,3,4096]{2,1,0:T(4,128)(2,1)}), bf16[64,3,4096]{2,1,0:T(4,128)(2,1)S(1)}, u32[]{:S(2)}, u32[]{:S(2)}) %all-to-all-start.5) | async-done | bytes 1572896 | tf_op jit(solution)/shard_map/all_to_all | solution.py:137
  566.6 9.9 %copy.2202 = bf16[1,192,4096]{1,0,2:T(2,128)(2,1)} copy(bf16[1,192,4096]{2,1,0:T(8,128)(2,1)} %bitcast.254) | data formatting | bytes 3145728 | tf_op jit(solution)/shard_map/broadcast_in_dim | solution.py:181
  576.4 25.0 %reduce.15 = bf16[4096,192]{1,0:T(8,128)(2,1)} reduce(bf16[4096,1,192]{2,1,0:T(2,128)(2,1)} %bitcast.244, bf16[]{:T(256)} %broadcast.341), dimensions={1}, to_apply=%bitcast.218.reduce_sub_computation | reduce | bytes 3145730
  601.4 5.5 reshape.479
  607.0 10.6 %all-to-all-start.7 = ((bf16[64,2,6144]{2,1,0:T(2,128)(2,1)}), bf16[64,2,6144]{2,1,0:T(2,128)(2,1)}, u32[]{:S(2)}, u32[]{:S(2)}) async-start(bf16[64,2,6144]{2,1,0:T(2,128)(2,1)} %reshape.479), calls=%async_computation.8 | async-start | bytes 3145728 | tf_op jit(solution)/shard_map/all_to_all | solution.py:181
  623.9 69.3 %all-to-all-done.7 = bf16[64,2,6144]{2,1,0:T(2,128)(2,1)} async-done(((bf16[64,2,6144]{2,1,0:T(2,128)(2,1)}), bf16[64,2,6144]{2,1,0:T(2,128)(2,1)}, u32[]{:S(2)}, u32[]{:S(2)}) %all-to-all-start.7) | async-done | bytes 1572896 | tf_op jit(solution)/shard_map/all_to_all | solution.py:181
  693.2 7.0 all-to-all-start.6
  700.2 10.7 %reshape.480 = bf16[4096,1,192]{2,1,0:T(2,128)(2,1)} reshape(bf16[64,2,6144]{2,1,0:T(2,128)(2,1)} %all-to-all-done.7) | data formatting | bytes 3145728
  717.7 15.4 %all-to-all-start.8 = ((bf16[64,192,64]{1,2,0:T(8,128)(2,1)}), bf16[64,192,64]{1,2,0:T(8,128)(2,1)}, u32[]{:S(2)}, u32[]{:S(2)}) async-start(bf16[64,192,64]{1,2,0:T(8,128)(2,1)} %copy.2204), calls=%async_computation.9 | async-start | bytes 4194304 | tf_op jit(solution)/shard_map/all_to_all | solution.py:185
  735.7 11.5 %psum.7 = f32[16,8]{1,0:T(8,128)S(1)} all-reduce(f32[16,8]{1,0:T(8,128)S(1)} %reduce_sum.100), channel_id=1, replica_groups=mesh['dp'=8,'expert'=64] {'dp'}, use_global_device_ids=true, to_apply=%region_17.18 | all-reduce | flops 128 | bytes 1024 | tf_op jit(solution)/shard_map/psum | solution.py:130
  749.5 81.1 %all-to-all-done.8 = bf16[64,192,64]{1,2,0:T(8,128)(2,1)} async-done(((bf16[64,192,64]{1,2,0:T(8,128)(2,1)}), bf16[64,192,64]{1,2,0:T(8,128)(2,1)}, u32[]{:S(2)}, u32[]{:S(2)}) %all-to-all-start.8) | async-done | bytes 1572896 | tf_op jit(solution)/shard_map/all_to_all | solution.py:185
  830.6 2.8 copy.2364
  833.4 4.4 copy.2206
  837.8 5.3 copy.2207
  843.1 5.1 fusion.2
  (224 shorter events, 93.5 us)
Async XLA Ops:
  7.2 62.0 %copy-start = (bf16[16,8,192]{2,1,0:T(8,128)(2,1)S(1)}, bf16[16,8,192]{2,1,0:T(8,128)(2,1)}, u32[]{:S(2)}) copy-start(bf16[16,8,192]{2,1,0:T(8,128)(2,1)} %param.14) | copy-start | bytes 147460
  44.6 19.0 %copy-start.29 = (s32[16,8]{0,1:T(8,128)S(1)}, s32[16,8]{0,1:T(8,128)}, u32[]{:S(2)}) copy-start(s32[16,8]{0,1:T(8,128)} %param.18) | copy-start | bytes 1540
  44.6 19.2 %copy-start.30 = (s32[16,8]{0,1:T(8,128)S(1)}, s32[16,8]{0,1:T(8,128)}, u32[]{:S(2)}) copy-start(s32[16,8]{0,1:T(8,128)} %param.19) | copy-start | bytes 1540
  44.6 19.5 %copy-start.35 = (s32[16,2]{0,1:T(2,128)S(1)}, s32[16,2]{0,1:T(2,128)}, u32[]{:S(2)}) copy-start(s32[16,2]{0,1:T(2,128)} %param.20) | copy-start | bytes 388
  44.6 20.1 %copy-start.36 = (s32[64]{0:T(128)S(1)}, s32[64]{0:T(128)}, u32[]{:S(2)}) copy-start(s32[64]{0:T(128)} %param.21) | copy-start | bytes 772
  44.6 95.1 %all-to-all-start.2 = ((bf16[64,2,6144]{2,1,0:T(2,128)(2,1)}), bf16[64,2,6144]{2,1,0:T(2,128)(2,1)S(1)}, u32[]{:S(2)}, u32[]{:S(2)}) async-start(bf16[64,2,6144]{2,1,0:T(2,128)(2,1)} %reshape.477), calls=%async_computation.2 | async-start | bytes 3145728 | tf_op jit(solution)/shard_map/all_to_all | solution.py:85
  68.4 85.8 %copy-start.7 = (pred[64,3]{1,0:T(8,128)(4,1)}, pred[64,3]{1,0:T(8,128)(4,1)S(1)}, u32[]{:S(2)}) copy-start(pred[64,3]{1,0:T(8,128)(4,1)S(1)} %le.50) | copy-start | bytes 580
  70.3 86.4 %copy-start.21 = (s32[64]{0:T(128)}, s32[64]{0:T(128)S(1)}, u32[]{:S(2)}) copy-start(s32[64]{0:T(128)S(1)} %get-tuple-element.530) | copy-start | bytes 772
  70.4 86.3 %copy-start.32 = (pred[64]{0:T(512)(128)(4,1)}, pred[64]{0:T(512)(128)(4,1)S(1)}, u32[]{:S(2)}) copy-start(pred[64]{0:T(512)(128)(4,1)S(1)} %broadcast_compare_fusion.4) | copy-start | bytes 196
  139.7 60.8 %all-to-all-start = ((s32[64,1,3]{2,1,0:T(1,128)}), s32[64,1,3]{2,1,0:T(1,128)S(1)}, u32[]{:S(2)}, u32[]{:S(2)}) async-start(s32[64,1,3]{2,1,0:T(1,128)} %bitcast.9), calls=%async_computation | async-start | bytes 65536 | tf_op jit(solution)/shard_map/all_to_all | solution.py:94
  200.5 30.0 %all-to-all-start.1 = ((bf16[64,3,192]{2,1,0:T(4,128)(2,1)}), bf16[64,3,192]{2,1,0:T(4,128)(2,1)S(1)}, u32[]{:S(2)}, u32[]{:S(2)}) async-start(bf16[64,3,192]{2,1,0:T(4,128)(2,1)} %select_select_fusion.1), calls=%async_computation.1 | async-start | bytes 262144 | tf_op jit(solution)/shard_map/all_to_all | solution.py:93
  216.8 117.6 %copy-start.2 = (bf16[1,192,4096]{2,1,0:T(8,128)(2,1)S(1)}, bf16[1,192,4096]{2,1,0:T(8,128)(2,1)}, u32[]{:S(2)}) copy-start(bf16[1,192,4096]{2,1,0:T(8,128)(2,1)} %param.15) | copy-start | bytes 4718596
  230.5 103.9 %all-to-all-start.3 = ((bf16[64,1,192,64]{2,3,1,0:T(8,128)(2,1)}), bf16[64,1,192,64]{2,3,1,0:T(8,128)(2,1)}, u32[]{:S(2)}, u32[]{:S(2)}) async-start(bf16[64,1,192,64]{2,3,1,0:T(8,128)(2,1)} %constant_dynamic-update-slice_fusion), calls=%async_computation.3 | async-start | bytes 4194304 | tf_op jit(solution)/shard_map/all_to_all | solution.py:11
  337.3 10.4 %copy-start.26 = (s32[128]{0:T(128)S(1)}, s32[128]{0:T(128)}, u32[]{:S(2)}) copy-start(s32[128]{0:T(128)} %copy-done.25) | copy-start | bytes 1540
  337.3 10.5 %copy-start.24 = (s32[128]{0:T(128)S(1)}, s32[128]{0:T(128)}, u32[]{:S(2)}) copy-start(s32[128]{0:T(128)} %copy-done.23) | copy-start | bytes 1540
  337.3 10.6 %copy-start.28 = (s32[128]{0:T(128)S(1)}, s32[128]{0:T(128)}, u32[]{:S(2)}) copy-start(s32[128]{0:T(128)} %copy-done.27) | copy-start | bytes 1540
  337.3 10.7 %copy-start.31 = (f32[16,8]{0,1:T(8,128)S(1)}, f32[16,8]{0,1:T(8,128)}, u32[]{:S(2)}) copy-start(f32[16,8]{0,1:T(8,128)} %param.16) | copy-start | bytes 1540
  337.4 10.9 %copy-start.12 = (s32[16,8]{1,0:T(8,128)S(1)}, s32[16,8]{1,0:T(8,128)}, u32[]{:S(2)}) copy-start(s32[16,8]{1,0:T(8,128)} %copy-done.11) | copy-start | bytes 1540
  337.4 11.1 %copy-start.17 = (bf16[16,512]{1,0:T(8,128)(2,1)S(1)}, bf16[16,512]{1,0:T(8,128)(2,1)}, u32[]{:S(2)}) copy-start(bf16[16,512]{1,0:T(8,128)(2,1)} %param.17) | copy-start | bytes 49156
  337.4 24.1 %copy-start.34 = (s32[128]{0:T(128)S(1)}, s32[128]{0:T(128)}, u32[]{:S(2)}) copy-start(s32[128]{0:T(128)} %get-tuple-element.536) | copy-start | bytes 1540
  337.4 107.9 %all-to-all-start.4 = ((bf16[64,3,4096]{2,1,0:T(4,128)(2,1)}), bf16[64,3,4096]{2,1,0:T(4,128)(2,1)}, u32[]{:S(2)}, u32[]{:S(2)}) async-start(bf16[64,3,4096]{2,1,0:T(4,128)(2,1)} %reshape.368), calls=%async_computation.4 | async-start | bytes 4194304 | tf_op jit(solution)/shard_map/all_to_all | solution.py:113
  348.1 100.3 %copy-start.9 = (f32[16,8]{1,0:T(8,128)}, f32[16,8]{1,0:T(8,128)S(1)}, u32[]{:S(2)}) copy-start(f32[16,8]{1,0:T(8,128)S(1)} %copy.2187) | copy-start | bytes 1540
  348.3 100.2 %copy-start.13 = (pred[16,8]{1,0:T(8,128)(4,1)}, pred[16,8]{1,0:T(8,128)(4,1)S(1)}, u32[]{:S(2)}) copy-start(pred[16,8]{1,0:T(8,128)(4,1)S(1)} %get-tuple-element.534) | copy-start | bytes 388
  348.3 100.2 %copy-start.15 = (pred[16,8]{1,0:T(8,128)(4,1)}, pred[16,8]{1,0:T(8,128)(4,1)S(1)}, u32[]{:S(2)}) copy-start(pred[16,8]{1,0:T(8,128)(4,1)S(1)} %get-tuple-element.535) | copy-start | bytes 388
  458.2 104.5 %all-to-all-start.5 = ((bf16[64,3,4096]{2,1,0:T(4,128)(2,1)}), bf16[64,3,4096]{2,1,0:T(4,128)(2,1)S(1)}, u32[]{:S(2)}, u32[]{:S(2)}) async-start(bf16[64,3,4096]{2,1,0:T(4,128)(2,1)} %select_select_fusion), calls=%async_computation.6 | async-start | bytes 4194304 | tf_op jit(solution)/shard_map/all_to_all | solution.py:137
  607.0 86.2 %all-to-all-start.7 = ((bf16[64,2,6144]{2,1,0:T(2,128)(2,1)}), bf16[64,2,6144]{2,1,0:T(2,128)(2,1)}, u32[]{:S(2)}, u32[]{:S(2)}) async-start(bf16[64,2,6144]{2,1,0:T(2,128)(2,1)} %reshape.479), calls=%async_computation.8 | async-start | bytes 3145728 | tf_op jit(solution)/shard_map/all_to_all | solution.py:181
  693.2 24.5 %all-to-all-start.6 = ((bf16[64,3,192]{2,1,0:T(4,128)(2,1)}), bf16[64,3,192]{2,1,0:T(4,128)(2,1)S(1)}, u32[]{:S(2)}, u32[]{:S(2)}) async-start(bf16[64,3,192]{2,1,0:T(4,128)(2,1)} %reshape.372), calls=%async_computation.7 | async-start | bytes 262144 | tf_op jit(solution)/shard_map/all_to_all | solution.py:158
  717.6 16.3 %copy-start.10 = (f32[16,8]{1,0:T(8,128)S(1)}, f32[16,8]{1,0:T(8,128)}, u32[]{:S(2)}) copy-start(f32[16,8]{1,0:T(8,128)} %copy-done.9) | copy-start | bytes 1540
  717.6 16.3 %copy-start.14 = (pred[16,8]{1,0:T(8,128)(4,1)S(1)}, pred[16,8]{1,0:T(8,128)(4,1)}, u32[]{:S(2)}) copy-start(pred[16,8]{1,0:T(8,128)(4,1)} %copy-done.13) | copy-start | bytes 388
  717.7 16.3 %copy-start.16 = (pred[16,8]{1,0:T(8,128)(4,1)S(1)}, pred[16,8]{1,0:T(8,128)(4,1)}, u32[]{:S(2)}) copy-start(pred[16,8]{1,0:T(8,128)(4,1)} %copy-done.15) | copy-start | bytes 388
  717.7 113.0 %all-to-all-start.8 = ((bf16[64,192,64]{1,2,0:T(8,128)(2,1)}), bf16[64,192,64]{1,2,0:T(8,128)(2,1)}, u32[]{:S(2)}, u32[]{:S(2)}) async-start(bf16[64,192,64]{1,2,0:T(8,128)(2,1)} %copy.2204), calls=%async_computation.9 | async-start | bytes 4194304 | tf_op jit(solution)/shard_map/all_to_all | solution.py:185
  733.1 115.1 %reduce-scatter.2.cloned.1.call-start = ((), (), s32[]{:S(2)}) async-start(), calls=%async_computation.10 | async-start | bytes 147456 | tf_op jit(solution)/shard_map/reduce_scatter | solution.py:126
  (13 other events, 56.2 us)
Sparse Core Ops, SparseCore 0:
  737.3 36.2 reduce-scatter.1
